TPU v7x, 32 devices: a whole 2x2x4 slice. The times are simulated.
32 devices in a mesh: row: 4 (over y, x), col: 8 (over z, core).
Axes of the slice: x: 2, y: 2, z: 4, core: 2. Of those that a mesh axis runs over, the one named last changes fastest.
Arguments:
- z_slab: float32 [1024, 1024], P('col', 'row'), may hold values from -6 to 6
- prev_factor: bfloat16 [1024, 32768], P('row', 'col'), may hold values from -0.03125 to 0.03125
- prev_solution: bfloat16 [1024, 32768], P(None, 'col'), may hold values from -6 to 6
- slab_factor: bfloat16 [1024, 1024], P('row'), may hold values from -0.09375 to 0.09375
- diag_inverse: bfloat16 [1024, 256], P('row'), may hold values from -1 to 2, as said below
Outputs:
- solved: float32 [1024, 1024], P('col', 'row')
Inputs may be any that keep to these rules, and one draw needn't show every extreme that they name: `diag_inverse`: each 256 x 256 block is lower triangular with its diagonal between 1 and 2.
All inputs are finite; a program needn't handle non-finite values.
Results may differ from a plain program's by a relative error of at most 0.0003.
Values sent between devices are 32-bit elements; how exact they have to be, the bound alone decides.
A program may use at most 64 MiB of HBM per device.

v0:
```python
import jax
import jax.numpy as jnp
from jax import lax
from jax.sharding import PartitionSpec as P


def spread(block, axis, owner):
    block = jnp.where(lax.axis_index(axis) == owner, block, jnp.zeros_like(block))
    return lax.psum(block, axis)


def precise_dot(left, right):
    return lax.dot_general(
        left,
        right,
        (((1,), (1,)), ((), ())),
        precision=lax.Precision.HIGHEST,
        preferred_element_type=jnp.float32,
    )


def on_device(z_slab, prev_factor, prev_solution, slab_factor, diag_inverse):
    row_count = z_slab.shape[0]
    block_width = diag_inverse.shape[1]
    block_rows = lax.axis_size("row")
    partial_value = lax.dot_general(
        prev_solution, prev_factor, (((1,), (1,)), ((), ())), preferred_element_type=jnp.float32
    )
    summed = lax.psum(partial_value, "col")
    fan_sum = lax.dynamic_slice_in_dim(summed, lax.axis_index("col") * row_count, row_count, 0)
    remainder = z_slab - fan_sum
    factor = slab_factor.astype(jnp.float32)
    inverse = diag_inverse.astype(jnp.float32)
    device_row = lax.axis_index("row")
    result = jnp.zeros((row_count, block_width), jnp.float32)
    updates = jnp.zeros((row_count, block_width), jnp.float32)

    def bcast_step(block_index, carry):
        result, updates = carry
        candidate = precise_dot(remainder - updates, inverse)
        arrived = spread(candidate, "row", block_index)
        result = jnp.where(device_row == block_index, arrived, result)
        columns = lax.dynamic_slice_in_dim(factor, block_index * block_width, block_width, 1)
        updates = updates + precise_dot(arrived, columns)
        return (result, updates)

    result, updates = lax.fori_loop(0, block_rows, bcast_step, (result, updates))
    return result


def solution(mesh):
    in_specs = (P("col", "row"), P("row", "col"), P(None, "col"), P("row", None), P("row", None))
    out_specs = P("col", "row")
    return jax.shard_map(
        on_device, mesh=mesh, in_specs=in_specs, out_specs=out_specs, check_vma=False
    )
```

profile of v0, /device:TPU:0, one launch (start us, length us, event | category | flops | bytes accessed | tf_op | source)
XLA Modules:
  0.0 277.1 jit_solution(165684188814202454)
XLA Ops:
  6.5 0.0 copy-start
  6.5 0.0 all-reduce.3.cloned.1.call-start
  6.5 1.6 copy-done
  8.1 6.8 %fusion.7 = f32[1024,256]{1,0:T(8,128)} fusion(bf16[1024,4096]{1,0:T(8,128)(2,1)} %param.9, bf16[256,4096]{1,0:T(8,128)(2,1)S(1)} %copy-done), kind=kOutput, calls=%fused_computation.11 | convolution fusion | flops 2147483648 | bytes 11534336 | tf_op jit(solution)/shard_map/dot_general | solution.py:26
  14.9 0.0 all-reduce.3.cloned.1.call-update
  14.9 1.1 convert_element_type.7
  16.1 0.9 convert_element_type.6
  17.0 59.6 %all-reduce.3.cloned.1.call-done = f32[1024,256]{1,0:T(8,128)} async-done(((f32[1024,256]{1,0:T(8,128)}), f32[1024,256]{1,0:T(8,128)}) %all-reduce.3.cloned.1.call-update) | async-done | bytes 1048592 | tf_op jit(solution)/shard_map/psum | solution.py:29
  76.6 1.6 dynamic-slice_subtract_fusion
  78.3 192.3 %while.16 = (s32[]{:T(128)}, f32[128,256]{1,0:T(8,128)}, f32[128,256]{1,0:T(8,128)S(1)}, s32[]{:T(128)}, f32[128,256]{1,0:T(8,128)}, /*index=5*/f32[256,256]{1,0...) while((s32[]{:T(128)}, f32[128,256]{1,0:T(8,128)}, ...), condition=%wide.region_3.4_spmd.clone, body=%wide.region_1.3_spmd.clone.sunk | while | flops 201588736 | bytes 2490639 | solution.py:47
  78.3 0.0 all-reduce.5.cloned.1.call-start
  78.3 1.9 convolution_select_fusion.2
  80.2 0.0 all-reduce.5.cloned.1.call-update
  80.3 42.7 %all-reduce.5.cloned.1.call-done = f32[128,256]{1,0:T(8,128)} async-done(((f32[128,256]{1,0:T(8,128)}), f32[128,256]{1,0:T(8,128)}) %all-reduce.5.cloned.1.call-update) | async-done | bytes 131088 | tf_op jit(solution)/shard_map/while/body/eval_jaxpr/psum | solution.py:9
  123.0 1.4 convolution_add_fusion.2
  124.3 1.6 select_select_fusion.2
  125.9 2.0 convolution_select_fusion.2
  127.9 0.0 all-reduce.5.cloned.1.call-update
  127.9 42.9 %all-reduce.5.cloned.1.call-done = f32[128,256]{1,0:T(8,128)} async-done(((f32[128,256]{1,0:T(8,128)}), f32[128,256]{1,0:T(8,128)}) %all-reduce.5.cloned.1.call-update) | async-done | bytes 131088 | tf_op jit(solution)/shard_map/while/body/eval_jaxpr/psum | solution.py:9
  170.8 1.4 convolution_add_fusion.2
  172.1 1.6 select_select_fusion.2
  173.7 0.0 all-reduce.5.cloned.1.call-start
  173.7 1.9 convolution_select_fusion.2
  175.7 0.0 all-reduce.5.cloned.1.call-update
  175.7 43.5 %all-reduce.5.cloned.1.call-done = f32[128,256]{1,0:T(8,128)} async-done(((f32[128,256]{1,0:T(8,128)}), f32[128,256]{1,0:T(8,128)}) %all-reduce.5.cloned.1.call-update) | async-done | bytes 131088 | tf_op jit(solution)/shard_map/while/body/eval_jaxpr/psum | solution.py:9
  219.2 1.4 convolution_add_fusion.2
  220.6 1.6 select_select_fusion.2
  222.2 1.9 convolution_select_fusion.2
  224.1 0.0 all-reduce.5.cloned.1.call-update
  224.2 43.4 %all-reduce.5.cloned.1.call-done = f32[128,256]{1,0:T(8,128)} async-done(((f32[128,256]{1,0:T(8,128)}), f32[128,256]{1,0:T(8,128)}) %all-reduce.5.cloned.1.call-update) | async-done | bytes 131088 | tf_op jit(solution)/shard_map/while/body/eval_jaxpr/psum | solution.py:9
  267.6 1.4 convolution_add_fusion.2
  269.0 1.6 select_select_fusion.2
  (4 shorter events, 0.0 us)
Async XLA Ops:
  6.5 1.6 copy-start
  6.5 70.1 %all-reduce.3.cloned.1.call-start = ((), (), s32[]{:S(2)}) async-start(), calls=%async_computation | async-start | bytes 2097152 | tf_op jit(solution)/shard_map/psum | solution.py:29
  78.3 44.7 %all-reduce.5.cloned.1.call-start = ((), (), s32[]{:S(2)}) async-start(), calls=%async_computation.1 | async-start | bytes 262144 | tf_op jit(solution)/shard_map/while/body/eval_jaxpr/psum | solution.py:9
  125.9 44.9 %all-reduce.5.cloned.1.call-start = ((), (), s32[]{:S(2)}) async-start(), calls=%async_computation.1 | async-start | bytes 262144 | tf_op jit(solution)/shard_map/while/body/eval_jaxpr/psum | solution.py:9
  173.7 45.5 %all-reduce.5.cloned.1.call-start = ((), (), s32[]{:S(2)}) async-start(), calls=%async_computation.1 | async-start | bytes 262144 | tf_op jit(solution)/shard_map/while/body/eval_jaxpr/psum | solution.py:9
  222.2 45.4 %all-reduce.5.cloned.1.call-start = ((), (), s32[]{:S(2)}) async-start(), calls=%async_computation.1 | async-start | bytes 262144 | tf_op jit(solution)/shard_map/while/body/eval_jaxpr/psum | solution.py:9
Sparse Core Ops, SparseCore 0:
  15.0 61.5 all-reduce.2
  82.0 40.9 all-reduce.4
  129.6 41.1 all-reduce.4
  177.1 42.0 all-reduce.4
  225.6 41.9 all-reduce.4
where the time goes:
time: 278 us; the launch traced here: 277 us
  waiting for transfers between devices  232 us (83%)
  matrix products  20 us (7%)
  between operations  13.1 us (5%)
  other arithmetic  10.1 us (4%)
    psum x4, waiting for transfers between devices, spread(): return lax.psum(block, axis)  173 us
    psum x1, waiting for transfers between devices, on_device(): summed = lax.psum(partial_value, 'col')  59.6 us
    dot_general x8, matrix products, precise_dot(): lax.dot_general(left, right, (((1,), (1,)), ((), ())), precision=lax.Prec...  13.2 us
    dot_general x1, matrix products, on_device(): lax.dot_general(prev_solution, prev_factor, (((1,), (1,)), ((), ())), pre...  6.76 us
    select_n x4, other arithmetic, bcast_step(): result = jnp.where(device_row == block_index, arrived, result)  6.36 us
  transfers between devices with their start and end apart: 5, of which 5 were waited for; matrix products, arithmetic and copies ran while one was open for 1% of the time, Pallas kernels for 0%

commit v1 on v0

--- a/solution.py
+++ b/solution.py
@@ -26,7 +26,11 @@
     partial_value = lax.dot_general(
         prev_solution, prev_factor, (((1,), (1,)), ((), ())), preferred_element_type=jnp.float32
     )
-    summed = lax.psum(partial_value, "col")
+    n_dev = lax.axis_size("col")
+    summed, reach = (partial_value, 1)
+    while reach < n_dev:
+        summed = summed + lax.ppermute(summed, "col", [(i, i ^ reach) for i in range(n_dev)])
+        reach = 2 * reach
     fan_sum = lax.dynamic_slice_in_dim(summed, lax.axis_index("col") * row_count, row_count, 0)
     remainder = z_slab - fan_sum
     factor = slab_factor.astype(jnp.float32)

time: 278 us -> 296 us (1.065)
  waiting for transfers between devices: 232 us -> 244 us
  starting transfers between devices: 0.01 us -> 6.3 us
    ppermute x0 -> x3, waiting for transfers between devices: none -> 69.3 us  [on_device(): lax.ppermute(summed, 'col', [(i, i ^ reach) for i in range(n_dev)])]
    psum x1 -> x0, waiting for transfers between devices: 59.6 us -> none  [on_device(): summed = lax.psum(partial_value, 'col')]
    ppermute x0 -> x3, starting transfers between devices: none -> 6.29 us  [on_device(): lax.ppermute(summed, 'col', [(i, i ^ reach) for i in range(n_dev)])]
  transfers between devices with their start and end apart: 5 -> 7, of which waited for: 5 -> 7; matrix products, arithmetic and copies ran while one was open for 1% -> 1% of each run, Pallas kernels for 0% -> 0%
where the time goes in v1:
time: 296 us
  waiting for transfers between devices  244 us (82%)
  matrix products  19 us (6%)
  between operations  13.1 us (4%)
  other arithmetic  11.4 us (4%)
  starting transfers between devices  6.3 us (2%)
    psum x4, waiting for transfers between devices, spread(): return lax.psum(block, axis)  175 us
    ppermute x3, waiting for transfers between devices, on_device(): lax.ppermute(summed, 'col', [(i, i ^ reach) for i in range(n_dev)])  69.3 us
    dot_general x8, matrix products, precise_dot(): lax.dot_general(left, right, (((1,), (1,)), ((), ())), precision=lax.Prec...  13.2 us
    select_n x4, other arithmetic, bcast_step(): result = jnp.where(device_row == block_index, arrived, result)  6.36 us
    ppermute x3, starting transfers between devices, on_device(): lax.ppermute(summed, 'col', [(i, i ^ reach) for i in range(n_dev)])  6.29 us
  transfers between devices with their start and end apart: 7, of which 7 were waited for; matrix products, arithmetic and copies ran while one was open for 1% of the time, Pallas kernels for 0%

profile of v1, /device:TPU:0, one launch (start us, length us, event | category | flops | bytes accessed | tf_op | source)
XLA Modules:
  0.0 295.7 jit_solution(5577902164604195173)
XLA Ops:
  6.5 1.6 copy-done
  8.1 5.7 %fusion.8 = f32[1024,256]{1,0:T(8,128)S(1)} fusion(bf16[1024,4096]{1,0:T(8,128)(2,1)} %param.9, bf16[256,4096]{1,0:T(8,128)(2,1)S(1)} %copy-done), kind=kOutput, calls=%fused_computation.12 | convolution fusion | flops 2147483648 | bytes 11534336 | tf_op jit(solution)/shard_map/dot_general | solution.py:26
  13.9 0.5 collective-permute-start
  14.4 2.3 collective-permute-done
  16.7 0.1 add.44
  16.8 3.0 %collective-permute-start.1 = (f32[1024,256]{1,0:T(8,128)S(1)}, f32[1024,256]{1,0:T(8,128)S(1)}, u32[]{:S(2)}, u32[]{:S(2)}) collective-permute-start(f32[1024,256]{1,0:T(8,128)S(1)} %add.44), channel_id=1, source_target_pairs={{0,2},{1,3},{2,0},{3,1},{4,6},{5,7},{6,4},{7,5},{8,10},{9,11},{10,... | collective-permute-start | bytes 3145736 | tf_op jit(solution)/shard_map/ppermute | solution.py:32
  19.8 23.5 %collective-permute-done.1 = f32[1024,256]{1,0:T(8,128)S(1)} collective-permute-done((f32[1024,256]{1,0:T(8,128)S(1)}, f32[1024,256]{1,0:T(8,128)S(1)}, u32[]{:S(2)}, u32[]{:S(2)}) %collective-permute-start.1) | collective-permute-done | bytes 1048608 | tf_op jit(solution)/shard_map/ppermute | solution.py:32
  43.3 1.1 add.45
  44.4 2.8 collective-permute-start.2
  47.2 1.1 convert_element_type.7
  48.3 0.9 convert_element_type.6
  49.2 43.5 %collective-permute-done.2 = f32[1024,256]{1,0:T(8,128)} collective-permute-done((f32[1024,256]{1,0:T(8,128)}, f32[1024,256]{1,0:T(8,128)}, u32[]{:S(2)}, u32[]{:S(2)}) %collective-permute-start.2) | collective-permute-done | bytes 1048608 | tf_op jit(solution)/shard_map/ppermute | solution.py:32
  92.8 1.7 fusion.7
  94.5 194.6 %while.16 = (s32[]{:T(128)}, f32[128,256]{1,0:T(8,128)}, f32[128,256]{1,0:T(8,128)S(1)}, s32[]{:T(128)}, f32[128,256]{1,0:T(8,128)}, /*index=5*/f32[256,256]{1,0...) while((s32[]{:T(128)}, f32[128,256]{1,0:T(8,128)}, ...), condition=%wide.region_2.3_spmd.clone, body=%wide.region_0.2_spmd.clone.sunk | while | flops 201588736 | bytes 2490639 | solution.py:51
  94.5 2.0 convolution_select_fusion.2
  96.4 0.0 all-reduce.2.cloned.1.call-update
  96.5 44.7 %all-reduce.2.cloned.1.call-done = f32[128,256]{1,0:T(8,128)} async-done(((f32[128,256]{1,0:T(8,128)}), f32[128,256]{1,0:T(8,128)}) %all-reduce.2.cloned.1.call-update) | async-done | bytes 131088 | tf_op jit(solution)/shard_map/while/body/eval_jaxpr/psum | solution.py:9
  141.2 1.4 convolution_add_fusion.2
  142.6 1.6 select_select_fusion.2
  144.2 2.0 convolution_select_fusion.2
  146.1 0.0 all-reduce.2.cloned.1.call-update
  146.2 42.9 %all-reduce.2.cloned.1.call-done = f32[128,256]{1,0:T(8,128)} async-done(((f32[128,256]{1,0:T(8,128)}), f32[128,256]{1,0:T(8,128)}) %all-reduce.2.cloned.1.call-update) | async-done | bytes 131088 | tf_op jit(solution)/shard_map/while/body/eval_jaxpr/psum | solution.py:9
  189.0 1.4 convolution_add_fusion.2
  190.4 1.6 select_select_fusion.2
  192.0 2.0 convolution_select_fusion.2
  194.0 43.8 %all-reduce.2.cloned.1.call-done = f32[128,256]{1,0:T(8,128)} async-done(((f32[128,256]{1,0:T(8,128)}), f32[128,256]{1,0:T(8,128)}) %all-reduce.2.cloned.1.call-update) | async-done | bytes 131088 | tf_op jit(solution)/shard_map/while/body/eval_jaxpr/psum | solution.py:9
  237.8 1.4 convolution_add_fusion.2
  239.1 1.6 select_select_fusion.2
  240.7 2.0 convolution_select_fusion.2
  242.7 43.4 %all-reduce.2.cloned.1.call-done = f32[128,256]{1,0:T(8,128)} async-done(((f32[128,256]{1,0:T(8,128)}), f32[128,256]{1,0:T(8,128)}) %all-reduce.2.cloned.1.call-update) | async-done | bytes 131088 | tf_op jit(solution)/shard_map/while/body/eval_jaxpr/psum | solution.py:9
  286.2 1.4 convolution_add_fusion.2
  287.5 1.6 select_select_fusion.2
  (9 shorter events, 0.0 us)
Async XLA Ops:
  6.5 1.6 copy-start
  13.9 2.8 collective-permute-start
  16.8 26.5 %collective-permute-start.1 = (f32[1024,256]{1,0:T(8,128)S(1)}, f32[1024,256]{1,0:T(8,128)S(1)}, u32[]{:S(2)}, u32[]{:S(2)}) collective-permute-start(f32[1024,256]{1,0:T(8,128)S(1)} %add.44), channel_id=1, source_target_pairs={{0,2},{1,3},{2,0},{3,1},{4,6},{5,7},{6,4},{7,5},{8,10},{9,11},{10,... | collective-permute-start | bytes 3145736 | tf_op jit(solution)/shard_map/ppermute | solution.py:32
  44.4 48.4 %collective-permute-start.2 = (f32[1024,256]{1,0:T(8,128)}, f32[1024,256]{1,0:T(8,128)}, u32[]{:S(2)}, u32[]{:S(2)}) collective-permute-start(f32[1024,256]{1,0:T(8,128)} %add.45), channel_id=1, source_target_pairs={{0,4},{1,5},{2,6},{3,7},{4,0},{5,1},{6,2},{7,3},{8,12},{9,13},{10,... | collective-permute-start | bytes 3145736 | tf_op jit(solution)/shard_map/ppermute | solution.py:32
  94.5 46.7 %all-reduce.2.cloned.1.call-start = ((), (), s32[]{:S(2)}) async-start(), calls=%async_computation | async-start | bytes 262144 | tf_op jit(solution)/shard_map/while/body/eval_jaxpr/psum | solution.py:9
  144.2 44.9 %all-reduce.2.cloned.1.call-start = ((), (), s32[]{:S(2)}) async-start(), calls=%async_computation | async-start | bytes 262144 | tf_op jit(solution)/shard_map/while/body/eval_jaxpr/psum | solution.py:9
  192.0 45.8 %all-reduce.2.cloned.1.call-start = ((), (), s32[]{:S(2)}) async-start(), calls=%async_computation | async-start | bytes 262144 | tf_op jit(solution)/shard_map/while/body/eval_jaxpr/psum | solution.py:9
  240.7 45.4 %all-reduce.2.cloned.1.call-start = ((), (), s32[]{:S(2)}) async-start(), calls=%async_computation | async-start | bytes 262144 | tf_op jit(solution)/shard_map/while/body/eval_jaxpr/psum | solution.py:9
Sparse Core Ops, SparseCore 0:
  98.2 42.9 all-reduce.1
  147.9 41.1 all-reduce.1
  195.7 42.0 all-reduce.1
  244.1 41.9 all-reduce.1
